TPU v7x, 512 devices: a whole 4x8x8 slice. The times are simulated.
512 devices in a mesh: tm: 64 (over x, z, core), region: 8 (over y).
Axes of the slice: x: 4, y: 8, z: 8, core: 2. Of those that a mesh axis runs over, the one named last changes fastest.
Arguments:
- activity: bfloat16 [6144, 131072], P('region', 'tm'), may hold values from -6 to 6
- test_matrix: bfloat16 [131072, 512], P('tm', 'region'), may hold values from -0.015625 to 0.015625
- basis_mix: float32 [512, 64], replicated, may hold values from -0.25 to 0.25
- recurrent: float32 [64, 64], replicated, may hold values from -0.75 to 0.75
- latent_bias: float32 [64], replicated, may hold values from -2 to 2
- readout: bfloat16 [6144, 64], P('region'), may hold values from -0.75 to 0.75
- region_in: bfloat16 [6144, 8], P('region'), may hold values from -0.21875 to 0.21875
- region_out: bfloat16 [6144, 8], P('region'), may hold values from -1 to 1
- region_of_block: int32 [48], replicated, may hold values from 0 to 7, never falling along the last dimension, each value on 1 to 12 neighbouring positions
- region_mask: int32 [8, 8], replicated, may hold values 0 or 1
Outputs:
- latents: float32 [64, 131072], P(None, 'tm')
- frame_loss: float32 [131072], P('tm')
- readout_score: float32 [6144, 64], P('region')
Inputs may be any that keep to these rules, and one draw needn't show every extreme that they name: `region_of_block`: blocks of one region are consecutive, every region holds at least one block, and no region holds more than 12 blocks.
All inputs are finite; a program needn't handle non-finite values.
Results may differ from a plain program's by a relative error of at most 0.0028.
Values may be sent and summed in bfloat16 or wider, within the bound.
No kernel may reach another device: no remote copies, remote signals or barrier semaphores. Data moves between devices by JAX's collectives and lax.ppermute only.
A program may use at most 64 MiB of HBM per device.

v0:
```python
import jax
import jax.numpy as jnp
from jax import lax
from jax.sharding import PartitionSpec as P

BLOCK = 128
precise = lax.Precision.HIGHEST
epsilon = 1e-05


def from_behind(block, axis, distance):
    devices = range(lax.axis_size(axis))
    route = [(i - distance, i) for i in devices if i - distance in devices]
    return lax.ppermute(block, axis, route)


def orthonormal(sketch, gram):
    lower = jnp.linalg.cholesky(gram)
    return jax.scipy.linalg.solve_triangular(lower, sketch.T, lower=True).T


def region_tables(block_regions, region_mask, region_in, region_out):
    regions = region_mask.shape[0]
    signal_width = region_in.shape[1]
    block_total = block_regions.shape[0]
    block_rows = region_in.shape[0] // block_total
    onehot = (block_regions[:, None] == jnp.arange(regions, dtype=jnp.int32)[None, :]).astype(
        jnp.float32
    )
    onehot = jnp.broadcast_to(onehot[:, None, :], (block_total, block_rows, regions)).reshape(
        block_total * block_rows, regions
    )
    allowed = jnp.dot(onehot, region_mask.astype(jnp.float32), precision=precise)
    region_feed = (onehot[:, :, None] * region_in.astype(jnp.float32)[:, None, :]).reshape(
        -1, regions * signal_width
    )
    spread = (allowed[:, :, None] * region_out.astype(jnp.float32)[:, None, :]).reshape(
        -1, regions * signal_width
    )
    return (region_feed.astype(jnp.bfloat16), spread.astype(jnp.bfloat16))


def local(
    activity,
    test_matrix,
    basis_mix,
    recurrent,
    latent_bias,
    readout,
    region_in,
    region_out,
    region_of_block,
    region_mask,
):
    neurons_here, frames_here = activity.shape
    contract = (((0,), (0,)), ((), ()))
    block_count = neurons_here // BLOCK
    my_blocks = lax.dynamic_slice_in_dim(
        region_of_block, lax.axis_index("region") * block_count, block_count
    )
    region_feed, spread = region_tables(my_blocks, region_mask, region_in, region_out)
    test_full = lax.all_gather(test_matrix, "region", axis=1, tiled=True)
    sketch_rows = lax.psum_scatter(
        jnp.dot(activity, test_full, preferred_element_type=jnp.float32),
        "tm",
        scatter_dimension=0,
        tiled=True,
    )
    gram = lax.psum(jnp.dot(sketch_rows.T, sketch_rows, precision=precise), ("tm", "region"))
    loading_rows = jnp.dot(orthonormal(sketch_rows, gram), basis_mix, precision=precise).astype(
        jnp.bfloat16
    )
    latent_part = lax.dot_general(
        lax.all_gather(loading_rows, "tm", axis=0, tiled=True),
        activity,
        contract,
        preferred_element_type=jnp.float32,
    )
    signal_part = lax.dot_general(
        region_feed, activity, contract, preferred_element_type=jnp.float32
    )
    latents, signals = lax.psum((latent_part, signal_part), "region")
    prior_latent, prior_signal = from_behind((latents[:, -1:], signals[:, -1:]), "tm", 1)
    lagged_latents = jnp.concatenate([prior_latent, latents[:, :-1]], axis=1)
    lagged_signals = jnp.concatenate([prior_signal, signals[:, :-1]], axis=1)
    hidden = jnp.tanh(jnp.dot(recurrent, lagged_latents, precision=precise) + latent_bias[:, None])
    predicted = jnp.dot(readout, hidden.astype(jnp.bfloat16), preferred_element_type=jnp.float32)
    predicted = predicted + jnp.dot(
        spread, lagged_signals.astype(jnp.bfloat16), preferred_element_type=jnp.float32
    )
    error = activity.astype(jnp.float32) - predicted
    squared = error * error
    cross, error_sq, hidden_sq = lax.psum(
        (
            jnp.dot(error, hidden.T, precision=precise),
            jnp.sum(squared, axis=1),
            jnp.sum(hidden * hidden, axis=1),
        ),
        "tm",
    )
    frame_sq = lax.psum(jnp.sum(squared, axis=0), "region")
    frames_all = frames_here * lax.axis_size("tm")
    frame_loss = frame_sq / (neurons_here * lax.axis_size("region"))
    readout_score = cross / jnp.sqrt(
        frames_all
        * (error_sq[:, None] / frames_all + epsilon)
        * (hidden_sq[None, :] / frames_all + epsilon)
    )
    return (latents, frame_loss, readout_score)


def solution(mesh):
    in_specs = (
        P("region", "tm"),
        P("tm", "region"),
        P(),
        P(),
        P(),
        P("region", None),
        P("region", None),
        P("region", None),
        P(),
        P(),
    )
    out_specs = (P(None, "tm"), P("tm"), P("region", None))
    return jax.shard_map(local, mesh=mesh, in_specs=in_specs, out_specs=out_specs, check_vma=False)
```

profile of v0, /device:TPU:8, one launch (start us, length us, event | category | flops | bytes accessed | tf_op | source)
XLA Modules:
  0.0 1049.4 jit_solution(13345600834286897948)
XLA Ops:
  8.0 50.1 %all-gather.3.cloned.1.call-done = bf16[2048,512]{0,1:T(8,128)(2,1)} async-done(((bf16[2048,64]{0,1:T(8,128)(2,1)}), bf16[2048,512]{0,1:T(8,128)(2,1)}) %all-gather.3.cloned.1.call-update) | async-done | bytes 2097168 | tf_op jit(solution)/shard_map/all_gather | solution.py:62
  58.1 5.5 fusion.73
  63.6 141.2 %fusion = f32[16,512]{1,0:T(8,128)S(1)} fusion(f32[768,512]{1,0:T(8,128)} %fusion.73), kind=kCustom, calls=%all-reduce-scatter | all-reduce-scatter fusion | flops 524289 | bytes 1607680
  204.8 1.3 collective-permute-start.17
  206.1 1.3 collective-permute-start.16
  207.4 1.3 collective-permute-start.15
  208.7 1.3 collective-permute-start.14
  210.0 1.3 collective-permute-start.13
  211.3 1.3 collective-permute-start.12
  212.7 11.6 %collective-permute-start.11 = (f32[16,512]{1,0:T(8,128)S(1)}, f32[16,512]{1,0:T(8,128)S(1)}, u32[]{:S(2)}, u32[]{:S(2)}) collective-permute-start(f32[16,512]{1,0:T(8,128)S(1)} %fusion), channel_id=1, source_target_pairs={{0,80},{8,88},{16,96},{24,104},{32,112},{40,120},{48,128},{56,136}... | collective-permute-start | bytes 98312
  224.3 1.9 collective-permute-start.10
  226.3 5.7 collective-permute-start.9
  231.9 1.5 collective-permute-start.8
  233.4 3.8 collective-permute-start.7
  237.3 4.1 collective-permute-start.6
  241.5 3.3 collective-permute-start.5
  244.8 2.7 collective-permute-start.4
  247.5 2.5 collective-permute-start.3
  250.1 2.0 collective-permute-start.2
  252.9 1.3 dynamic-slice.7
  254.9 23.2 %concatenate.21 = f32[268,512]{1,0:T(8,128)} concatenate(f32[12,512]{1,0:T(8,128)S(1)} %collective-permute-done.17, f32[16,512]{1,0:T(8,128)S(1)} %collective-permute-done.16, f32[16,512]{1,0:T(8,128)S(1)} %collective-permute-done.15, f32[16,512]{1,0:T(8,128)S(1)} %collective-permute-done.14, f32[16,512]{1,0:T(8,128)S(1)} %collective-permute-done.13, ...), dimensions={0} | concatenate | bytes 1097728
  278.1 2.9 fusion.50
  281.6 1.5 fusion.26
  283.0 1.4 dynamic-slice_bitcast_fusion
  284.4 262.1 %all-reduce.9.cloned.1.call-done = f32[512,512]{0,1:T(8,128)} async-done(((f32[512,512]{0,1:T(8,128)}), f32[512,512]{0,1:T(8,128)}) %all-reduce.9.cloned.1.call-update) | async-done | bytes 1048592 | tf_op jit(solution)/shard_map/psum | solution.py:69
  546.5 2.6 copy.25
  549.1 1.8 fusion.4
  551.8 11.7 %cholesky.104 = f32[128,128]{1,0:T(8,128)S(1)} custom-call(f32[128,128]{1,0:T(8,128)S(1)} %cholesky.266), custom_call_target="Cholesky" | custom-call | tf_op jit(solution)/shard_map/jit(cholesky)/cholesky | solution.py:18
  563.6 9.8 custom-call.31
  573.4 1.1 cholesky.224
  574.5 1.9 constant_dynamic-update-slice_fusion.3
  576.5 1.3 convolution_subtract_fusion
  578.4 12.5 %cholesky.217 = f32[128,128]{1,0:T(8,128)S(1)} custom-call(f32[128,128]{1,0:T(8,128)} %cholesky.270), custom_call_target="Cholesky" | custom-call | tf_op jit(solution)/shard_map/jit(cholesky)/cholesky | solution.py:18
  591.6 10.8 %custom-call.32 = f32[1,128,128]{1,2,0:T(8,128)S(1)} custom-call(f32[1,128,128]{2,1,0:T(8,128)} %get-tuple-element.31), custom_call_target="InvertDiagBlocksLowerTriangular" | custom-call | tf_op jit(solution)/shard_map/jit(cholesky)/cholesky | solution.py:18
  603.3 1.4 convolution_subtract_fusion.1
  604.8 11.7 %cholesky.238 = f32[128,128]{1,0:T(8,128)S(1)} custom-call(f32[128,128]{1,0:T(8,128)S(1)} %cholesky.275), custom_call_target="Cholesky" | custom-call | tf_op jit(solution)/shard_map/jit(cholesky)/cholesky | solution.py:18
  617.8 9.8 custom-call.33
  628.4 1.4 convolution_subtract_fusion.2
  629.9 11.9 %cholesky.255 = f32[128,128]{1,0:T(8,128)S(1)} custom-call(f32[128,128]{1,0:T(8,128)S(1)} %convolution_subtract_fusion.2), custom_call_target="Cholesky" | custom-call | tf_op jit(solution)/shard_map/jit(cholesky)/cholesky | solution.py:18
  646.3 2.3 select_select_fusion
  648.6 14.4 %while.1 = (s32[]{:T(128)}, f32[512,512]{1,0:T(8,128)}, s32[4,2]{0,1:T(2,128)S(1)}, f32[4,128,128]{2,1,0:T(8,128)}, s32[]{:T(128)}) while((s32[]{:T(128)}, f32[512,512]{1,0:T(8,128)}, s32[4,2]{0,1:T(2,128)S(1)}, f32[4,128,128]{2,1,0:T(8,128)}, s32[]{:T(128)}) %tuple.34), condition=%wide.while_cond, body=%wide.while_body.sunk | while | flops 2 | bytes 132205 | solution.py:19
  649.3 3.0 bitcast_dynamic-update-slice_fusion.2
  652.9 3.0 bitcast_dynamic-update-slice_fusion.2
  656.5 3.0 bitcast_dynamic-update-slice_fusion.2
  660.1 2.9 bitcast_dynamic-update-slice_fusion.2
  663.0 40.1 %custom-call.34 = f32[4,128,128]{1,2,0:T(8,128)S(1)} custom-call(f32[4,128,128]{2,1,0:T(8,128)} %get-tuple-element.10), custom_call_target="InvertDiagBlocksLowerTriangular" | custom-call | tf_op jit(solution)/shard_map/jit(_solve_triangular)/triangular_solve | solution.py:19
  705.9 1.1 fusion.19
  707.9 1.3 fusion.14
  710.3 43.1 %all-gather = bf16[64,12,64]{2,1,0:T(8,128)(2,1)S(1)} all-gather(bf16[1,12,64]{2,1,0:T(8,128)(2,1)S(1)} %fusion.3), channel_id=1, replica_groups=mesh['tm'=64,'region'=8] {'tm'}, dimensions={0}, use_global_device_ids=true | all-gather | bytes 99840 | tf_op jit(solution)/shard_map/all_gather | solution.py:74
  754.2 2.4 fusion.74
  756.7 35.5 %all-reduce.14 = bf16[64,2048]{1,0:T(8,128)(2,1)S(1)} all-reduce(f32[64,2048]{1,0:T(8,128)} %fusion.26), channel_id=1, replica_groups=mesh['tm'=64,'region'=8] {'region'}, use_global_device_ids=true, to_apply=%region_11.12 | all-reduce | flops 131072 | bytes 786432 | tf_op jit(solution)/shard_map/psum | solution.py:82
  792.8 1.9 collective-permute-start.1
  794.7 36.6 %all-reduce.11.cloned.1.call-done = f32[64,2048]{1,0:T(8,128)} async-done(((f32[64,2048]{1,0:T(8,128)}), f32[64,2048]{1,0:T(8,128)}) %all-reduce.11.cloned.1.call-update) | async-done | bytes 524304 | tf_op jit(solution)/shard_map/psum | solution.py:82
  831.3 1.4 slice.142
  832.7 2.1 collective-permute-start
  835.7 2.8 copy.26
  838.6 1.9 multiply_reduce_fusion.2
  840.5 2.1 fusion.12
  842.6 2.5 multiply_reduce_fusion
  845.2 4.8 fusion.75
  850.0 129.4 %all-reduce.3 = (f32[64]{0:T(128)S(1)}, f32[768]{0:T(1024)S(1)}) all-reduce(f32[64]{0:T(128)S(1)} %get-tuple-element.38, f32[768]{0:T(1024)S(1)} %get-tuple-element.11), channel_id=1, replica_groups=mesh['tm'=64,'region'=8] {'tm'}, use_global_device_ids=true, to_apply=%region_18.19 | all-reduce | flops 832 | bytes 6656 | tf_op jit(solution)/shard_map/psum | solution.py:93
  979.4 15.0 %psum.52 = f32[2048]{0:T(1024)S(1)} all-reduce(f32[2048]{0:T(1024)S(1)} %get-tuple-element.12), channel_id=1, replica_groups=mesh['tm'=64,'region'=8] {'region'}, use_global_device_ids=true, to_apply=%region_13.14 | all-reduce | flops 2048 | bytes 16384 | tf_op jit(solution)/shard_map/psum | solution.py:101
  995.0 45.1 %all-reduce.13.cloned.1.call-done = f32[768,64]{0,1:T(8,128)} async-done(((f32[768,64]{0,1:T(8,128)}), f32[768,64]{0,1:T(8,128)}) %all-reduce.13.cloned.1.call-update) | async-done | bytes 196624 | tf_op jit(solution)/shard_map/psum | solution.py:93
  1040.1 1.7 rsqrt_multiply_fusion
  (102 shorter events, 20.9 us)
Async XLA Ops:
  7.2 702.9 %copy-start = (f32[512,64]{0,1:T(8,128)S(1)}, f32[512,64]{0,1:T(8,128)}, u32[]{:S(2)}) copy-start(f32[512,64]{0,1:T(8,128)} %param.12) | copy-start | bytes 393220
  7.2 50.9 %all-gather.3.cloned.1.call-start = ((), (), s32[]{:S(2)}) async-start(), calls=%async_computation | async-start | bytes 2359296 | tf_op jit(solution)/shard_map/all_gather | solution.py:62
  7.9 204.7 %copy-start.16 = (s32[48]{0:T(128)S(1)}, s32[48]{0:T(128)}, u32[]{:S(2)}) copy-start(s32[48]{0:T(128)} %param.18) | copy-start | bytes 580
  7.9 538.6 %all-reduce.9.cloned.1.call-start = ((), (), s32[]{:S(2)}) async-start(), calls=%async_computation.1 | async-start | bytes 2097152 | tf_op jit(solution)/shard_map/psum | solution.py:69
  63.6 218.0 %copy-start.1 = (bf16[768,2048]{1,0:T(8,128)(2,1)S(1)}, bf16[768,2048]{1,0:T(8,128)(2,1)}, u32[]{:S(2)}) copy-start(bf16[768,2048]{1,0:T(8,128)(2,1)} %param.10) | copy-start | bytes 9437188
  204.8 6.5 collective-permute-start.17
  206.1 6.6 collective-permute-start.16
  207.4 16.9 %collective-permute-start.15 = (f32[16,512]{1,0:T(8,128)S(1)}, f32[16,512]{1,0:T(8,128)S(1)}, u32[]{:S(2)}, u32[]{:S(2)}) collective-permute-start(f32[16,512]{1,0:T(8,128)S(1)} %fusion), channel_id=1, source_target_pairs={{0,112},{8,120},{16,128},{24,136},{32,144},{40,152},{48,160},{56,1... | collective-permute-start | bytes 98312
  208.7 17.5 %collective-permute-start.14 = (f32[16,512]{1,0:T(8,128)S(1)}, f32[16,512]{1,0:T(8,128)S(1)}, u32[]{:S(2)}, u32[]{:S(2)}) collective-permute-start(f32[16,512]{1,0:T(8,128)S(1)} %fusion), channel_id=1, source_target_pairs={{0,104},{8,112},{16,120},{24,128},{32,136},{40,144},{48,152},{56,1... | collective-permute-start | bytes 98312
  210.0 21.9 %collective-permute-start.13 = (f32[16,512]{1,0:T(8,128)S(1)}, f32[16,512]{1,0:T(8,128)S(1)}, u32[]{:S(2)}, u32[]{:S(2)}) collective-permute-start(f32[16,512]{1,0:T(8,128)S(1)} %fusion), channel_id=1, source_target_pairs={{0,96},{8,104},{16,112},{24,120},{32,128},{40,136},{48,144},{56,15... | collective-permute-start | bytes 98312
  211.3 22.1 %collective-permute-start.12 = (f32[16,512]{1,0:T(8,128)S(1)}, f32[16,512]{1,0:T(8,128)S(1)}, u32[]{:S(2)}, u32[]{:S(2)}) collective-permute-start(f32[16,512]{1,0:T(8,128)S(1)} %fusion), channel_id=1, source_target_pairs={{0,88},{8,96},{16,104},{24,112},{32,120},{40,128},{48,136},{56,144... | collective-permute-start | bytes 98312
  212.7 24.6 %collective-permute-start.11 = (f32[16,512]{1,0:T(8,128)S(1)}, f32[16,512]{1,0:T(8,128)S(1)}, u32[]{:S(2)}, u32[]{:S(2)}) collective-permute-start(f32[16,512]{1,0:T(8,128)S(1)} %fusion), channel_id=1, source_target_pairs={{0,80},{8,88},{16,96},{24,104},{32,112},{40,120},{48,128},{56,136}... | collective-permute-start | bytes 98312
  224.3 17.2 %collective-permute-start.10 = (f32[16,512]{1,0:T(8,128)S(1)}, f32[16,512]{1,0:T(8,128)S(1)}, u32[]{:S(2)}, u32[]{:S(2)}) collective-permute-start(f32[16,512]{1,0:T(8,128)S(1)} %fusion), channel_id=1, source_target_pairs={{0,72},{8,80},{16,88},{24,96},{32,104},{40,112},{48,120},{56,128},... | collective-permute-start | bytes 98312
  226.3 18.6 %collective-permute-start.9 = (f32[16,512]{1,0:T(8,128)S(1)}, f32[16,512]{1,0:T(8,128)S(1)}, u32[]{:S(2)}, u32[]{:S(2)}) collective-permute-start(f32[16,512]{1,0:T(8,128)S(1)} %fusion), channel_id=1, source_target_pairs={{0,64},{8,72},{16,80},{24,88},{32,96},{40,104},{48,112},{56,120},{... | collective-permute-start | bytes 98312
  231.9 15.6 %collective-permute-start.8 = (f32[16,512]{1,0:T(8,128)S(1)}, f32[16,512]{1,0:T(8,128)S(1)}, u32[]{:S(2)}, u32[]{:S(2)}) collective-permute-start(f32[16,512]{1,0:T(8,128)S(1)} %fusion), channel_id=1, source_target_pairs={{0,56},{8,64},{16,72},{24,80},{32,88},{40,96},{48,104},{56,112},{6... | collective-permute-start | bytes 98312
  233.4 16.7 %collective-permute-start.7 = (f32[16,512]{1,0:T(8,128)S(1)}, f32[16,512]{1,0:T(8,128)S(1)}, u32[]{:S(2)}, u32[]{:S(2)}) collective-permute-start(f32[16,512]{1,0:T(8,128)S(1)} %fusion), channel_id=1, source_target_pairs={{0,48},{8,56},{16,64},{24,72},{32,80},{40,88},{48,96},{56,104},{64... | collective-permute-start | bytes 98312
  237.3 14.9 %copy-start.11 = (f32[6,8]{1,0:T(8,128)}, f32[6,8]{1,0:T(8,128)S(1)}, u32[]{:S(2)}) copy-start(f32[6,8]{1,0:T(8,128)S(1)} %fusion.66) | copy-start | bytes 580
  237.3 12.7 %copy-start.5 = (f32[16,512]{1,0:T(8,128)}, f32[16,512]{1,0:T(8,128)S(1)}, u32[]{:S(2)}) copy-start(f32[16,512]{1,0:T(8,128)S(1)} %collective-permute-done.11) | copy-start | bytes 98308
  237.3 17.5 %collective-permute-start.6 = (f32[16,512]{1,0:T(8,128)S(1)}, f32[16,512]{1,0:T(8,128)}, u32[]{:S(2)}, u32[]{:S(2)}) collective-permute-start(f32[16,512]{1,0:T(8,128)S(1)} %fusion), channel_id=1, source_target_pairs={{0,40},{8,48},{16,56},{24,64},{32,72},{40,80},{48,88},{56,96},{64,... | collective-permute-start | bytes 98312
  241.5 10.6 %copy-start.6 = (f32[16,512]{1,0:T(8,128)}, f32[16,512]{1,0:T(8,128)S(1)}, u32[]{:S(2)}) copy-start(f32[16,512]{1,0:T(8,128)S(1)} %collective-permute-done.10) | copy-start | bytes 98308
  241.5 13.4 %collective-permute-start.5 = (f32[16,512]{1,0:T(8,128)S(1)}, f32[16,512]{1,0:T(8,128)}, u32[]{:S(2)}, u32[]{:S(2)}) collective-permute-start(f32[16,512]{1,0:T(8,128)S(1)} %fusion), channel_id=1, source_target_pairs={{0,32},{8,40},{16,48},{24,56},{32,64},{40,72},{48,80},{56,88},{64,... | collective-permute-start | bytes 98312
  244.8 7.4 copy-start.7
  244.8 10.1 collective-permute-start.4
  247.5 4.7 copy-start.8
  247.5 7.4 collective-permute-start.3
  250.1 2.1 copy-start.9
  250.1 4.8 collective-permute-start.2
  281.0 550.3 %all-reduce.11.cloned.1.call-start = ((), (), s32[]{:S(2)}) async-start(), calls=%async_computation.2 | async-start | bytes 1048576 | tf_op jit(solution)/shard_map/psum | solution.py:82
  550.9 1.0 copy-start.3
  709.2 125.7 %copy-start.12 = (f32[6,8]{1,0:T(8,128)S(1)}, f32[6,8]{1,0:T(8,128)}, u32[]{:S(2)}) copy-start(f32[6,8]{1,0:T(8,128)} %copy-done.11) | copy-start | bytes 580
  709.2 125.7 %copy-start.15 = (s32[8,8]{1,0:T(8,128)S(1)}, s32[8,8]{1,0:T(8,128)}, u32[]{:S(2)}) copy-start(s32[8,8]{1,0:T(8,128)} %param.19) | copy-start | bytes 772
  756.6 283.5 %all-reduce.13.cloned.1.call-start = ((), (), s32[]{:S(2)}) async-start(), calls=%async_computation.3 | async-start | bytes 393216 | tf_op jit(solution)/shard_map/psum | solution.py:93
  792.8 49.8 %collective-permute-start.1 = (bf16[64,1]{1,0:T(8,128)(2,1)}, bf16[64,1]{1,0:T(8,128)(2,1)}, u32[]{:S(2)}, u32[]{:S(2)}) collective-permute-start(bf16[64,1]{1,0:T(8,128)(2,1)} %slice.144), channel_id=1, source_target_pairs={{0,8},{8,16},{16,24},{24,32},{32,40},{40,48},{48,56},{56,64},{64,7... | collective-permute-start | bytes 392 | tf_op jit(solution)/shard_map/ppermute | solution.py:14
  832.7 5.8 collective-permute-start
  835.7 2.8 copy-start.13
  835.7 2.8 copy-start.14
  840.5 2.1 copy-start.2
  840.5 2.1 copy-start.10
  845.1 196.6 %copy-start.4 = (f32[64,2048]{1,0:T(8,128)S(1)}, f32[64,2048]{1,0:T(8,128)}, u32[]{:S(2)}) copy-start(f32[64,2048]{1,0:T(8,128)} %all-reduce.11.cloned.1.call-done) | copy-start | bytes 1572868
Sparse Core Ops, SparseCore 0:
  10.1 47.9 all-gather.2
  281.1 265.3 all-reduce.8
  756.7 74.5 all-reduce.10
  850.1 189.9 all-reduce.12
where the time goes:
time: 1060 us; the launch traced here: 1050 us
  waiting for transfers between devices  395 us (37%)
  blocking collectives  364 us (34%)
  other arithmetic  130 us (12%)
  local copies, waits for them, and re-layouts  52.3 us (5%)
  starting transfers between devices  51.6 us (5%)
  matrix products  39.4 us (4%)
  between operations  17.7 us (2%)
    psum x1, waiting for transfers between devices, local(): lax.psum(jnp.dot(sketch_rows.T, sketch_rows, precision=precise), ('tm', '...  262 us
    unnamed x1, blocking collectives  141 us
    psum x1, blocking collectives, local(): lax.psum((jnp.dot(error, hidden.T, precision=precise), jnp.sum(squared, a...  129 us
    another operation x14, other arithmetic, orthonormal(): lower = jnp.linalg.cholesky(gram)  82.2 us
    all_gather x1, waiting for transfers between devices, local(): test_full = lax.all_gather(test_matrix, 'region', axis=1, tiled=True)  50.1 us
    unnamed x16, starting transfers between devices  47 us
    psum x1, waiting for transfers between devices, local(): lax.psum((jnp.dot(error, hidden.T, precision=precise), jnp.sum(squared, a...  45.1 us
    all_gather x1, blocking collectives, local(): lax.all_gather(loading_rows, 'tm', axis=0, tiled=True)  43.1 us
  transfers between devices with their start and end apart: 22, of which 4 were waited for; matrix products, arithmetic and copies ran while one was open for 1% of the time, Pallas kernels for 0%

commit v1 on v0

--- a/solution.py
+++ b/solution.py
@@ -71,7 +71,9 @@
         jnp.bfloat16
     )
     latent_part = lax.dot_general(
-        lax.all_gather(loading_rows, "tm", axis=0, tiled=True),
+        jnp.concatenate(
+            lax.all_to_all(jnp.stack([loading_rows] * lax.axis_size("tm")), "tm", 0, 0), axis=0
+        ),
         activity,
         contract,
         preferred_element_type=jnp.float32,

time: 1060 us -> 999 us (0.942)
  blocking collectives: 364 us -> 323 us
  local copies, waits for them, and re-layouts: 52.3 us -> 30.1 us
    all_gather x1 -> x0, blocking collectives: 43.1 us -> none  [local(): lax.all_gather(loading_rows, 'tm', axis=0, tiled=True)]
    unnamed x40 -> x29, local copies, waits for them, and re-layouts: 29.9 us -> 9.25 us
  transfers between devices with their start and end apart: 22 -> 23, of which waited for: 4 -> 5; matrix products, arithmetic and copies ran while one was open for 1% -> 2% of each run, Pallas kernels for 0% -> 0%
where the time goes in v1:
time: 999 us; the launch traced here: 994 us
  waiting for transfers between devices  403 us (40%)
  blocking collectives  323 us (32%)
  other arithmetic  128 us (13%)
  starting transfers between devices  55.9 us (6%)
  matrix products  36.4 us (4%)
  local copies, waits for them, and re-layouts  30.1 us (3%)
  between operations  17.7 us (2%)
    psum x1, waiting for transfers between devices, local(): lax.psum(jnp.dot(sketch_rows.T, sketch_rows, precision=precise), ('tm', '...  265 us
    unnamed x1, blocking collectives  141 us
    psum x1, blocking collectives, local(): lax.psum((jnp.dot(error, hidden.T, precision=precise), jnp.sum(squared, a...  129 us
    another operation x14, other arithmetic, orthonormal(): lower = jnp.linalg.cholesky(gram)  80.9 us
    all_gather x1, waiting for transfers between devices, local(): test_full = lax.all_gather(test_matrix, 'region', axis=1, tiled=True)  50.1 us
    psum x1, waiting for transfers between devices, local(): lax.psum((jnp.dot(error, hidden.T, precision=precise), jnp.sum(squared, a...  45.5 us
    unnamed x16, starting transfers between devices  45.5 us
    another operation x3, other arithmetic, orthonormal(): return jax.scipy.linalg.solve_triangular(lower, sketch.T, lower=True).T  42.5 us
  transfers between devices with their start and end apart: 23, of which 5 were waited for; matrix products, arithmetic and copies ran while one was open for 2% of the time, Pallas kernels for 0%

profile of v1, /device:TPU:8, one launch (start us, length us, event | category | flops | bytes accessed | tf_op | source)
XLA Modules:
  0.0 993.7 jit_solution(606710493597999385)
XLA Ops:
  8.0 50.1 %all-gather.2.cloned.1.call-done = bf16[2048,512]{0,1:T(8,128)(2,1)} async-done(((bf16[2048,64]{0,1:T(8,128)(2,1)}), bf16[2048,512]{0,1:T(8,128)(2,1)}) %all-gather.2.cloned.1.call-update) | async-done | bytes 2097168 | tf_op jit(solution)/shard_map/all_gather | solution.py:62
  58.1 4.4 fusion.72
  62.4 140.5 %fusion = f32[16,512]{1,0:T(8,128)S(1)} fusion(f32[768,512]{1,0:T(8,128)S(1)} %fusion.72), kind=kCustom, calls=%all-reduce-scatter | all-reduce-scatter fusion | flops 524289 | bytes 1607680
  203.0 1.3 collective-permute-start.17
  204.3 1.3 collective-permute-start.16
  205.6 1.3 collective-permute-start.15
  206.9 1.3 collective-permute-start.14
  208.2 1.3 collective-permute-start.13
  209.5 1.3 collective-permute-start.12
  210.8 11.6 %collective-permute-start.11 = (f32[16,512]{1,0:T(8,128)S(1)}, f32[16,512]{1,0:T(8,128)S(1)}, u32[]{:S(2)}, u32[]{:S(2)}) collective-permute-start(f32[16,512]{1,0:T(8,128)S(1)} %fusion), channel_id=1, source_target_pairs={{0,80},{8,88},{16,96},{24,104},{32,112},{40,120},{48,128},{56,136}... | collective-permute-start | bytes 98312
  222.4 1.9 collective-permute-start.10
  224.4 5.7 collective-permute-start.9
  230.0 1.5 collective-permute-start.8
  231.5 3.8 collective-permute-start.7
  235.4 3.5 collective-permute-start.6
  238.9 2.7 collective-permute-start.5
  241.7 2.7 collective-permute-start.4
  244.4 2.1 collective-permute-start.3
  246.5 2.2 collective-permute-start.2
  249.4 1.3 dynamic-slice.7
  251.4 2.2 concatenate.21
  253.6 2.1 fusion.49
  257.1 265.4 %all-reduce.9.cloned.1.call-done = f32[512,512]{0,1:T(8,128)} async-done(((f32[512,512]{0,1:T(8,128)}), f32[512,512]{0,1:T(8,128)}) %all-reduce.9.cloned.1.call-update) | async-done | bytes 1048592 | tf_op jit(solution)/shard_map/psum | solution.py:69
  522.5 1.6 copy.25
  524.1 1.4 fusion.3
  525.6 11.7 %cholesky.104 = f32[128,128]{1,0:T(8,128)S(1)} custom-call(f32[128,128]{1,0:T(8,128)S(1)} %cholesky.266), custom_call_target="Cholesky" | custom-call | tf_op jit(solution)/shard_map/jit(cholesky)/cholesky | solution.py:18
  537.3 9.8 custom-call.31
  547.1 1.2 cholesky.224
  548.3 1.0 constant_dynamic-update-slice_fusion.3
  549.7 11.7 %cholesky.217 = f32[128,128]{1,0:T(8,128)S(1)} custom-call(f32[128,128]{1,0:T(8,128)S(1)} %cholesky.270), custom_call_target="Cholesky" | custom-call | tf_op jit(solution)/shard_map/jit(cholesky)/cholesky | solution.py:18
  562.1 10.3 %custom-call.32 = f32[1,128,128]{1,2,0:T(8,128)S(1)} custom-call(f32[1,128,128]{2,1,0:T(8,128)S(1)} %get-tuple-element.31), custom_call_target="InvertDiagBlocksLowerTriangular" | custom-call | tf_op jit(solution)/shard_map/jit(cholesky)/cholesky | solution.py:18
  573.3 1.6 convolution_subtract_fusion.1
  574.9 11.7 %cholesky.238 = f32[128,128]{1,0:T(8,128)S(1)} custom-call(f32[128,128]{1,0:T(8,128)S(1)} %cholesky.275), custom_call_target="Cholesky" | custom-call | tf_op jit(solution)/shard_map/jit(cholesky)/cholesky | solution.py:18
  587.9 9.8 custom-call.33
  598.5 1.4 convolution_subtract_fusion.2
  600.0 11.9 %cholesky.255 = f32[128,128]{1,0:T(8,128)S(1)} custom-call(f32[128,128]{1,0:T(8,128)S(1)} %convolution_subtract_fusion.2), custom_call_target="Cholesky" | custom-call | tf_op jit(solution)/shard_map/jit(cholesky)/cholesky | solution.py:18
  616.3 2.3 select_select_fusion
  618.6 13.7 %while.1 = (s32[]{:T(128)}, f32[512,512]{1,0:T(8,128)}, s32[4,2]{0,1:T(2,128)S(1)}, f32[4,128,128]{2,1,0:T(8,128)}, s32[]{:T(128)}) while((s32[]{:T(128)}, f32[512,512]{1,0:T(8,128)}, s32[4,2]{0,1:T(2,128)S(1)}, f32[4,128,128]{2,1,0:T(8,128)}, s32[]{:T(128)}) %tuple.34), condition=%wide.while_cond, body=%wide.while_body.sunk | while | flops 2 | bytes 132205 | solution.py:19
  619.2 2.8 bitcast_dynamic-update-slice_fusion.2
  622.7 2.8 bitcast_dynamic-update-slice_fusion.2
  626.1 2.8 bitcast_dynamic-update-slice_fusion.2
  629.6 2.8 bitcast_dynamic-update-slice_fusion.2
  632.3 40.1 %custom-call.34 = f32[4,128,128]{1,2,0:T(8,128)S(1)} custom-call(f32[4,128,128]{2,1,0:T(8,128)} %get-tuple-element.10), custom_call_target="InvertDiagBlocksLowerTriangular" | custom-call | tf_op jit(solution)/shard_map/jit(_solve_triangular)/triangular_solve | solution.py:19
  675.2 1.1 fusion.18
  677.2 1.3 fusion.13
  680.5 6.5 all-to-all-start
  687.0 2.2 fusion.25
  689.2 7.7 all-to-all-done
  696.9 1.1 reshape.116
  698.8 2.4 fusion.73
  701.3 37.6 %all-reduce.14 = bf16[64,2048]{1,0:T(8,128)(2,1)S(1)} all-reduce(f32[64,2048]{1,0:T(8,128)} %fusion.25), channel_id=1, replica_groups=mesh['tm'=64,'region'=8] {'region'}, use_global_device_ids=true, to_apply=%region_11.12 | all-reduce | flops 131072 | bytes 786432 | tf_op jit(solution)/shard_map/psum | solution.py:84
  739.6 1.9 collective-permute-start.1
  741.5 33.8 %all-reduce.11.cloned.1.call-done = f32[64,2048]{1,0:T(8,128)} async-done(((f32[64,2048]{1,0:T(8,128)}), f32[64,2048]{1,0:T(8,128)}) %all-reduce.11.cloned.1.call-update) | async-done | bytes 524304 | tf_op jit(solution)/shard_map/psum | solution.py:84
  775.3 1.4 slice.142
  776.7 1.9 collective-permute-start
  779.5 3.0 copy.26
  782.5 1.9 multiply_reduce_fusion.2
  784.5 2.1 fusion.11
  786.6 2.5 multiply_reduce_fusion
  789.1 4.8 fusion.74
  793.9 129.4 %all-reduce.3 = (f32[64]{0:T(128)S(1)}, f32[768]{0:T(1024)S(1)}) all-reduce(f32[64]{0:T(128)S(1)} %get-tuple-element.38, f32[768]{0:T(1024)S(1)} %get-tuple-element.11), channel_id=1, replica_groups=mesh['tm'=64,'region'=8] {'tm'}, use_global_device_ids=true, to_apply=%region_18.19 | all-reduce | flops 832 | bytes 6656 | tf_op jit(solution)/shard_map/psum | solution.py:95
  923.4 15.0 %psum.52 = f32[2048]{0:T(1024)S(1)} all-reduce(f32[2048]{0:T(1024)S(1)} %get-tuple-element.12), channel_id=1, replica_groups=mesh['tm'=64,'region'=8] {'region'}, use_global_device_ids=true, to_apply=%region_13.14 | all-reduce | flops 2048 | bytes 16384 | tf_op jit(solution)/shard_map/psum | solution.py:103
  939.0 45.5 %all-reduce.13.cloned.1.call-done = f32[768,64]{0,1:T(8,128)} async-done(((f32[768,64]{0,1:T(8,128)}), f32[768,64]{0,1:T(8,128)}) %all-reduce.13.cloned.1.call-update) | async-done | bytes 196624 | tf_op jit(solution)/shard_map/psum | solution.py:95
  984.4 1.7 rsqrt_multiply_fusion
  (94 shorter events, 21.0 us)
Async XLA Ops:
  7.2 672.2 %copy-start = (f32[512,64]{0,1:T(8,128)S(1)}, f32[512,64]{0,1:T(8,128)}, u32[]{:S(2)}) copy-start(f32[512,64]{0,1:T(8,128)} %param.12) | copy-start | bytes 393220
  7.2 50.9 %all-gather.2.cloned.1.call-start = ((), (), s32[]{:S(2)}) async-start(), calls=%async_computation.1 | async-start | bytes 2359296 | tf_op jit(solution)/shard_map/all_gather | solution.py:62
  7.9 240.8 %copy-start.6 = (bf16[768,8]{0,1:T(8,128)(2,1)S(1)}, bf16[768,8]{0,1:T(8,128)(2,1)}, u32[]{:S(2)}) copy-start(bf16[768,8]{0,1:T(8,128)(2,1)} %param.16) | copy-start | bytes 36868
  7.9 243.4 %copy-start.10 = (s32[48]{0:T(128)S(1)}, s32[48]{0:T(128)}, u32[]{:S(2)}) copy-start(s32[48]{0:T(128)} %param.18) | copy-start | bytes 580
  7.9 514.6 %all-reduce.9.cloned.1.call-start = ((), (), s32[]{:S(2)}) async-start(), calls=%async_computation.2 | async-start | bytes 2097152 | tf_op jit(solution)/shard_map/psum | solution.py:69
  203.0 6.5 collective-permute-start.17
  204.3 6.5 collective-permute-start.16
  205.6 16.8 %collective-permute-start.15 = (f32[16,512]{1,0:T(8,128)S(1)}, f32[16,512]{1,0:T(8,128)S(1)}, u32[]{:S(2)}, u32[]{:S(2)}) collective-permute-start(f32[16,512]{1,0:T(8,128)S(1)} %fusion), channel_id=1, source_target_pairs={{0,112},{8,120},{16,128},{24,136},{32,144},{40,152},{48,160},{56,1... | collective-permute-start | bytes 98312
  206.9 17.4 %collective-permute-start.14 = (f32[16,512]{1,0:T(8,128)S(1)}, f32[16,512]{1,0:T(8,128)S(1)}, u32[]{:S(2)}, u32[]{:S(2)}) collective-permute-start(f32[16,512]{1,0:T(8,128)S(1)} %fusion), channel_id=1, source_target_pairs={{0,104},{8,112},{16,120},{24,128},{32,136},{40,144},{48,152},{56,1... | collective-permute-start | bytes 98312
  208.2 21.8 %collective-permute-start.13 = (f32[16,512]{1,0:T(8,128)S(1)}, f32[16,512]{1,0:T(8,128)S(1)}, u32[]{:S(2)}, u32[]{:S(2)}) collective-permute-start(f32[16,512]{1,0:T(8,128)S(1)} %fusion), channel_id=1, source_target_pairs={{0,96},{8,104},{16,112},{24,120},{32,128},{40,136},{48,144},{56,15... | collective-permute-start | bytes 98312
  209.5 22.0 %collective-permute-start.12 = (f32[16,512]{1,0:T(8,128)S(1)}, f32[16,512]{1,0:T(8,128)S(1)}, u32[]{:S(2)}, u32[]{:S(2)}) collective-permute-start(f32[16,512]{1,0:T(8,128)S(1)} %fusion), channel_id=1, source_target_pairs={{0,88},{8,96},{16,104},{24,112},{32,120},{40,128},{48,136},{56,144... | collective-permute-start | bytes 98312
  210.8 24.5 %collective-permute-start.11 = (f32[16,512]{1,0:T(8,128)S(1)}, f32[16,512]{1,0:T(8,128)S(1)}, u32[]{:S(2)}, u32[]{:S(2)}) collective-permute-start(f32[16,512]{1,0:T(8,128)S(1)} %fusion), channel_id=1, source_target_pairs={{0,80},{8,88},{16,96},{24,104},{32,112},{40,120},{48,128},{56,136}... | collective-permute-start | bytes 98312
  222.4 16.5 %collective-permute-start.10 = (f32[16,512]{1,0:T(8,128)S(1)}, f32[16,512]{1,0:T(8,128)S(1)}, u32[]{:S(2)}, u32[]{:S(2)}) collective-permute-start(f32[16,512]{1,0:T(8,128)S(1)} %fusion), channel_id=1, source_target_pairs={{0,72},{8,80},{16,88},{24,96},{32,104},{40,112},{48,120},{56,128},... | collective-permute-start | bytes 98312
  224.4 17.3 %collective-permute-start.9 = (f32[16,512]{1,0:T(8,128)S(1)}, f32[16,512]{1,0:T(8,128)S(1)}, u32[]{:S(2)}, u32[]{:S(2)}) collective-permute-start(f32[16,512]{1,0:T(8,128)S(1)} %fusion), channel_id=1, source_target_pairs={{0,64},{8,72},{16,80},{24,88},{32,96},{40,104},{48,112},{56,120},{... | collective-permute-start | bytes 98312
  230.0 14.3 %collective-permute-start.8 = (f32[16,512]{1,0:T(8,128)S(1)}, f32[16,512]{1,0:T(8,128)S(1)}, u32[]{:S(2)}, u32[]{:S(2)}) collective-permute-start(f32[16,512]{1,0:T(8,128)S(1)} %fusion), channel_id=1, source_target_pairs={{0,56},{8,64},{16,72},{24,80},{32,88},{40,96},{48,104},{56,112},{6... | collective-permute-start | bytes 98312
  231.5 15.0 %collective-permute-start.7 = (f32[16,512]{1,0:T(8,128)S(1)}, f32[16,512]{1,0:T(8,128)S(1)}, u32[]{:S(2)}, u32[]{:S(2)}) collective-permute-start(f32[16,512]{1,0:T(8,128)S(1)} %fusion), channel_id=1, source_target_pairs={{0,48},{8,56},{16,64},{24,72},{32,80},{40,88},{48,96},{56,104},{64... | collective-permute-start | bytes 98312
  235.4 16.0 %collective-permute-start.6 = (f32[16,512]{1,0:T(8,128)S(1)}, f32[16,512]{1,0:T(8,128)S(1)}, u32[]{:S(2)}, u32[]{:S(2)}) collective-permute-start(f32[16,512]{1,0:T(8,128)S(1)} %fusion), channel_id=1, source_target_pairs={{0,40},{8,48},{16,56},{24,64},{32,72},{40,80},{48,88},{56,96},{64,... | collective-permute-start | bytes 98312
  238.9 12.5 %collective-permute-start.5 = (f32[16,512]{1,0:T(8,128)S(1)}, f32[16,512]{1,0:T(8,128)S(1)}, u32[]{:S(2)}, u32[]{:S(2)}) collective-permute-start(f32[16,512]{1,0:T(8,128)S(1)} %fusion), channel_id=1, source_target_pairs={{0,32},{8,40},{16,48},{24,56},{32,64},{40,72},{48,80},{56,88},{64,... | collective-permute-start | bytes 98312
  241.7 9.7 collective-permute-start.4
  244.4 7.0 collective-permute-start.3
  246.5 4.9 collective-permute-start.2
  525.6 46.8 %copy-start.3 = (f32[512,512]{1,0:T(8,128)}, f32[512,512]{1,0:T(8,128)S(1)}, u32[]{:S(2)}) copy-start(f32[512,512]{1,0:T(8,128)S(1)} %fusion.3) | copy-start | bytes 3145732
  573.3 113.7 %copy-start.1 = (bf16[768,2048]{1,0:T(8,128)(2,1)S(1)}, bf16[768,2048]{1,0:T(8,128)(2,1)}, u32[]{:S(2)}) copy-start(bf16[768,2048]{1,0:T(8,128)(2,1)} %param.10) | copy-start | bytes 9437188
  680.5 16.5 %all-to-all-start = ((bf16[64,2,384]{2,1,0:T(2,128)(2,1)}), bf16[64,2,384]{2,1,0:T(2,128)(2,1)}, u32[]{:S(2)}, u32[]{:S(2)}) async-start(bf16[64,2,384]{2,1,0:T(2,128)(2,1)} %reshape.115), calls=%async_computation | async-start | bytes 196608 | tf_op jit(solution)/shard_map/all_to_all | solution.py:75
  686.9 88.3 %all-reduce.11.cloned.1.call-start = ((), (), s32[]{:S(2)}) async-start(), calls=%async_computation.3 | async-start | bytes 1048576 | tf_op jit(solution)/shard_map/psum | solution.py:84
  689.2 89.4 %copy-start.9 = (s32[8,8]{1,0:T(8,128)S(1)}, s32[8,8]{1,0:T(8,128)}, u32[]{:S(2)}) copy-start(s32[8,8]{1,0:T(8,128)} %param.19) | copy-start | bytes 772
  701.2 283.2 %all-reduce.13.cloned.1.call-start = ((), (), s32[]{:S(2)}) async-start(), calls=%async_computation.4 | async-start | bytes 393216 | tf_op jit(solution)/shard_map/psum | solution.py:95
  739.6 46.9 %collective-permute-start.1 = (bf16[64,1]{1,0:T(8,128)(2,1)}, bf16[64,1]{1,0:T(8,128)(2,1)}, u32[]{:S(2)}, u32[]{:S(2)}) collective-permute-start(bf16[64,1]{1,0:T(8,128)(2,1)} %slice.144), channel_id=1, source_target_pairs={{0,8},{8,16},{16,24},{24,32},{32,40},{40,48},{48,56},{56,64},{64,7... | collective-permute-start | bytes 392 | tf_op jit(solution)/shard_map/ppermute | solution.py:14
  776.7 5.8 collective-permute-start
  779.5 3.0 copy-start.7
  779.5 3.0 copy-start.8
  784.4 2.1 copy-start.2
  784.4 2.1 copy-start.5
  789.1 197.1 %copy-start.4 = (f32[64,2048]{1,0:T(8,128)S(1)}, f32[64,2048]{1,0:T(8,128)}, u32[]{:S(2)}) copy-start(f32[64,2048]{1,0:T(8,128)} %all-reduce.11.cloned.1.call-done) | copy-start | bytes 1572868
Sparse Core Ops, SparseCore 0:
  10.1 47.9 all-gather.1
  255.8 266.6 all-reduce.8
  701.3 73.8 all-reduce.10
  794.0 190.3 all-reduce.12
